TPU v7x, 32 devices: a whole 2x2x4 slice. The times are simulated.
32 devices in a mesh: row: 4 (over y, x), col: 8 (over z, core).
Axes of the slice: x: 2, y: 2, z: 4, core: 2. Of those that a mesh axis runs over, the one named last changes fastest.
Arguments:
- density: float32 [32, 7, 128, 128], P(('row', 'col')), as said below
- pattern: int32 [32, 12], P(('row', 'col')), may hold values from 0 to 31, as said below
Outputs:
- purified: float32 [32, 7, 128, 128], P(('row', 'col'))
Inputs may be any that keep to these rules, and one draw needn't show every extreme that they name: `pattern`: row I lists the block columns (I + o) mod 32 for o = -6..6 in rising order of o, all but one o; the omitted o is nonzero and of magnitude 3 or less, and row (I + o) mod 32 omits -o. density[I, 0] is symmetric, and density[I, t] is zero where (I + t) mod 32 is not listed in row I of pattern.
All inputs are finite; a program needn't handle non-finite values.
Results may differ from a plain program's by a relative error of at most 0.0001.
Values sent between devices are 32-bit elements; how exact they have to be, the bound alone decides.
A program may use at most 64 MiB of HBM per device.

v0:
```python
import jax
import jax.numpy as jnp
from jax import lax
from jax.sharding import PartitionSpec as P

REACH = 6


def from_behind(block, axis, distance):
    devices = range(lax.axis_size(axis))
    route = [((i - distance) % len(devices), i) for i in devices]
    return lax.ppermute(block, axis, route)


def fetch_rows(local_band):
    rows_above = []
    rows_below = []
    upward = local_band
    downward = local_band
    for distance in range(1, REACH + 1):
        upward = from_behind(upward[1:], ("row", "col"), 1)
        downward = from_behind(downward[: REACH + 1 - distance], ("row", "col"), -1)
        rows_above.append(upward)
        rows_below.append(downward)
    return (rows_above, rows_below)


def make_upper(local_band, rows_above, rows_below):

    def upper_block(offset, width):
        if offset == 0:
            return local_band[width]
        if offset < 0:
            return rows_above[-offset - 1][width + offset]
        return rows_below[offset - 1][width]

    return upper_block


def left_operand(upper_block, inner):
    if inner >= 0:
        return (upper_block(0, inner), 1)
    return (upper_block(inner, -inner), 0)


def right_operand(upper_block, inner, target):
    if target >= inner:
        return (upper_block(inner, target - inner), 0)
    return (upper_block(target, inner - target), 1)


def band_product(upper_left, upper_right):
    results = []
    for target in range(REACH + 1):
        total = None
        for inner in range(target - REACH, REACH + 1):
            left_block, left_dim = left_operand(upper_left, inner)
            right_block, right_dim = right_operand(upper_right, inner, target)
            term = lax.dot_general(
                left_block,
                right_block,
                (((left_dim,), (right_dim,)), ((), ())),
                precision=lax.Precision.HIGHEST,
                preferred_element_type=jnp.float32,
            )
            total = term if total is None else total + term
        results.append(total)
    return jnp.stack(results, axis=0)


def on_device(density, pattern):
    local_band = density[0]
    total_rows = lax.axis_size("row") * lax.axis_size("col")
    position = lax.axis_index("row") * lax.axis_size("col") + lax.axis_index("col")
    columns = (position + jnp.arange(REACH + 1, dtype=jnp.int32)) % total_rows
    flags = jnp.any(pattern[0][None, :] == columns[:, None], axis=1).astype(jnp.float32)[
        :, None, None
    ]
    above_p, below_p = fetch_rows(local_band)
    upper_p = make_upper(local_band, above_p, below_p)
    square = flags * band_product(upper_p, upper_p)
    above_s, below_s = fetch_rows(square)
    upper_s = make_upper(square, above_s, below_s)
    cube = flags * band_product(upper_p, upper_s)
    return (3.0 * square - 2.0 * cube)[None]


def solution(mesh):
    return jax.shard_map(
        on_device,
        mesh=mesh,
        in_specs=(P(("row", "col"), None, None, None), P(("row", "col"), None)),
        out_specs=P(("row", "col"), None, None, None),
        check_vma=False,
    )
```

profile of v0, /device:TPU:0, one launch (start us, length us, event | category | flops | bytes accessed | tf_op | source)
XLA Modules:
  0.0 130.1 jit_solution(12379357456183350727)
XLA Ops:
  0.0 1.2 slice_bitcast_fusion
  1.7 6.0 %collective-permute-start.6 = (f32[6,128,128]{2,1,0:T(8,128)S(1)}, f32[6,128,128]{2,1,0:T(8,128)S(1)}, u32[]{:S(2)}, u32[]{:S(2)}) collective-permute-start(f32[6,128,128]{2,1,0:T(8,128)S(1)} %get-tuple-element.7), channel_id=1, source_target_pairs={{1,0},{2,1},{3,2},{4,3},{5,4},{6,5},{7,6},{8,7},{9,8},{10,9},{11,1... | collective-permute-start | bytes 1179656 | tf_op jit(solution)/shard_map/ppermute | solution.py:12
  8.8 0.6 copy-done.1
  10.1 4.6 %collective-permute-done = f32[6,128,128]{2,1,0:T(8,128)S(1)} collective-permute-done((f32[6,128,128]{2,1,0:T(8,128)S(1)}, f32[6,128,128]{2,1,0:T(8,128)S(1)}, u32[]{:S(2)}, u32[]{:S(2)}) %collective-permute-start) | collective-permute-done | bytes 393248 | tf_op jit(solution)/shard_map/ppermute | solution.py:12
  14.8 5.4 %collective-permute-start.7 = (f32[5,128,128]{2,1,0:T(8,128)S(1)}, f32[5,128,128]{2,1,0:T(8,128)S(1)}, u32[]{:S(2)}, u32[]{:S(2)}) collective-permute-start(f32[5,128,128]{2,1,0:T(8,128)S(1)} %slice.679), channel_id=1, source_target_pairs={{1,0},{2,1},{3,2},{4,3},{5,4},{6,5},{7,6},{8,7},{9,8},{10,9},{11,1... | collective-permute-start | bytes 983048 | tf_op jit(solution)/shard_map/ppermute | solution.py:12
  23.4 3.4 %collective-permute-done.1 = f32[5,128,128]{2,1,0:T(8,128)S(1)} collective-permute-done((f32[5,128,128]{2,1,0:T(8,128)S(1)}, f32[5,128,128]{2,1,0:T(8,128)S(1)}, u32[]{:S(2)}, u32[]{:S(2)}) %collective-permute-start.1) | collective-permute-done | bytes 327712 | tf_op jit(solution)/shard_map/ppermute | solution.py:12
  26.9 0.7 collective-permute-done.7
  27.6 5.7 %collective-permute-start.8 = (f32[4,128,128]{2,1,0:T(8,128)S(1)}, f32[4,128,128]{2,1,0:T(8,128)S(1)}, u32[]{:S(2)}, u32[]{:S(2)}) collective-permute-start(f32[4,128,128]{2,1,0:T(8,128)S(1)} %slice.688), channel_id=1, source_target_pairs={{1,0},{2,1},{3,2},{4,3},{5,4},{6,5},{7,6},{8,7},{9,8},{10,9},{11,1... | collective-permute-start | bytes 786440 | tf_op jit(solution)/shard_map/ppermute | solution.py:12
  36.7 0.6 collective-permute-done.2
  37.4 5.4 %collective-permute-start.9 = (f32[3,128,128]{2,1,0:T(8,128)S(1)}, f32[3,128,128]{2,1,0:T(8,128)S(1)}, u32[]{:S(2)}, u32[]{:S(2)}) collective-permute-start(f32[3,128,128]{2,1,0:T(8,128)S(1)} %slice.695), channel_id=1, source_target_pairs={{1,0},{2,1},{3,2},{4,3},{5,4},{6,5},{7,6},{8,7},{9,8},{10,9},{11,1... | collective-permute-start | bytes 589832 | tf_op jit(solution)/shard_map/ppermute | solution.py:12
  45.7 0.6 collective-permute-done.3
  46.4 5.4 %collective-permute-start.10 = (f32[2,128,128]{2,1,0:T(8,128)S(1)}, f32[2,128,128]{2,1,0:T(8,128)S(1)}, u32[]{:S(2)}, u32[]{:S(2)}) collective-permute-start(f32[2,128,128]{2,1,0:T(8,128)S(1)} %slice.700), channel_id=1, source_target_pairs={{1,0},{2,1},{3,2},{4,3},{5,4},{6,5},{7,6},{8,7},{9,8},{10,9},{11,1... | collective-permute-start | bytes 393224 | tf_op jit(solution)/shard_map/ppermute | solution.py:12
  53.8 0.6 collective-permute-done.4
  54.5 5.6 %collective-permute-start.11 = (f32[1,128,128]{2,1,0:T(8,128)S(1)}, f32[1,128,128]{2,1,0:T(8,128)S(1)}, u32[]{:S(2)}, u32[]{:S(2)}) collective-permute-start(f32[1,128,128]{2,1,0:T(8,128)S(1)} %slice.701), channel_id=1, source_target_pairs={{1,0},{2,1},{3,2},{4,3},{5,4},{6,5},{7,6},{8,7},{9,8},{10,9},{11,1... | collective-permute-start | bytes 196616 | tf_op jit(solution)/shard_map/ppermute | solution.py:12
  61.3 0.5 collective-permute-done.5
  66.8 3.8 %collective-permute-start.18 = (f32[6,128,128]{2,1,0:T(8,128)S(1)}, f32[6,128,128]{2,1,0:T(8,128)S(1)}, u32[]{:S(2)}, u32[]{:S(2)}) collective-permute-start(f32[6,128,128]{2,1,0:T(8,128)S(1)} %get-tuple-element.5), channel_id=1, source_target_pairs={{1,0},{2,1},{3,2},{4,3},{5,4},{6,5},{7,6},{8,7},{9,8},{10,9},{11,1... | collective-permute-start | bytes 1179656 | tf_op jit(solution)/shard_map/ppermute | solution.py:12
  70.9 10.6 %collective-permute-done.12 = f32[6,128,128]{2,1,0:T(8,128)S(1)} collective-permute-done((f32[6,128,128]{2,1,0:T(8,128)S(1)}, f32[6,128,128]{2,1,0:T(8,128)S(1)}, u32[]{:S(2)}, u32[]{:S(2)}) %collective-permute-start.12) | collective-permute-done | bytes 393248 | tf_op jit(solution)/shard_map/ppermute | solution.py:12
  81.7 5.4 %collective-permute-start.19 = (f32[5,128,128]{2,1,0:T(8,128)S(1)}, f32[5,128,128]{2,1,0:T(8,128)S(1)}, u32[]{:S(2)}, u32[]{:S(2)}) collective-permute-start(f32[5,128,128]{2,1,0:T(8,128)S(1)} %slice.736), channel_id=1, source_target_pairs={{1,0},{2,1},{3,2},{4,3},{5,4},{6,5},{7,6},{8,7},{9,8},{10,9},{11,1... | collective-permute-start | bytes 983048 | tf_op jit(solution)/shard_map/ppermute | solution.py:12
  90.3 1.5 %collective-permute-done.13 = f32[5,128,128]{2,1,0:T(8,128)S(1)} collective-permute-done((f32[5,128,128]{2,1,0:T(8,128)S(1)}, f32[5,128,128]{2,1,0:T(8,128)S(1)}, u32[]{:S(2)}, u32[]{:S(2)}) %collective-permute-start.13) | collective-permute-done | bytes 327712 | tf_op jit(solution)/shard_map/ppermute | solution.py:12
  92.3 5.7 %collective-permute-start.20 = (f32[4,128,128]{2,1,0:T(8,128)S(1)}, f32[4,128,128]{2,1,0:T(8,128)S(1)}, u32[]{:S(2)}, u32[]{:S(2)}) collective-permute-start(f32[4,128,128]{2,1,0:T(8,128)S(1)} %slice.745), channel_id=1, source_target_pairs={{1,0},{2,1},{3,2},{4,3},{5,4},{6,5},{7,6},{8,7},{9,8},{10,9},{11,1... | collective-permute-start | bytes 786440 | tf_op jit(solution)/shard_map/ppermute | solution.py:12
  101.9 5.6 %collective-permute-start.21 = (f32[3,128,128]{2,1,0:T(8,128)S(1)}, f32[3,128,128]{2,1,0:T(8,128)S(1)}, u32[]{:S(2)}, u32[]{:S(2)}) collective-permute-start(f32[3,128,128]{2,1,0:T(8,128)S(1)} %slice.752), channel_id=1, source_target_pairs={{1,0},{2,1},{3,2},{4,3},{5,4},{6,5},{7,6},{8,7},{9,8},{10,9},{11,1... | collective-permute-start | bytes 589832 | tf_op jit(solution)/shard_map/ppermute | solution.py:12
  110.7 5.6 %collective-permute-start.22 = (f32[2,128,128]{2,1,0:T(8,128)S(1)}, f32[2,128,128]{2,1,0:T(8,128)S(1)}, u32[]{:S(2)}, u32[]{:S(2)}) collective-permute-start(f32[2,128,128]{2,1,0:T(8,128)S(1)} %slice.757), channel_id=1, source_target_pairs={{1,0},{2,1},{3,2},{4,3},{5,4},{6,5},{7,6},{8,7},{9,8},{10,9},{11,1... | collective-permute-start | bytes 393224 | tf_op jit(solution)/shard_map/ppermute | solution.py:12
  118.7 5.5 %collective-permute-start.23 = (f32[1,128,128]{2,1,0:T(8,128)S(1)}, f32[1,128,128]{2,1,0:T(8,128)S(1)}, u32[]{:S(2)}, u32[]{:S(2)}) collective-permute-start(f32[1,128,128]{2,1,0:T(8,128)S(1)} %slice.758), channel_id=1, source_target_pairs={{1,0},{2,1},{3,2},{4,3},{5,4},{6,5},{7,6},{8,7},{9,8},{10,9},{11,1... | collective-permute-start | bytes 196616 | tf_op jit(solution)/shard_map/ppermute | solution.py:12
  129.2 0.9 multiply_subtract_fusion
  (202 shorter events, 38.2 us)
Async XLA Ops:
  1.2 13.4 %collective-permute-start = (f32[6,128,128]{2,1,0:T(8,128)S(1)}, f32[6,128,128]{2,1,0:T(8,128)S(1)}, u32[]{:S(2)}, u32[]{:S(2)}) collective-permute-start(f32[6,128,128]{2,1,0:T(8,128)S(1)} %get-tuple-element.8), channel_id=1, source_target_pairs={{31,0},{0,1},{1,2},{2,3},{3,4},{4,5},{5,6},{6,7},{7,8},{8,9},{9,10... | collective-permute-start | bytes 1179656 | tf_op jit(solution)/shard_map/ppermute | solution.py:12
  1.7 13.0 %collective-permute-start.6 = (f32[6,128,128]{2,1,0:T(8,128)S(1)}, f32[6,128,128]{2,1,0:T(8,128)S(1)}, u32[]{:S(2)}, u32[]{:S(2)}) collective-permute-start(f32[6,128,128]{2,1,0:T(8,128)S(1)} %get-tuple-element.7), channel_id=1, source_target_pairs={{1,0},{2,1},{3,2},{4,3},{5,4},{6,5},{7,6},{8,7},{9,8},{10,9},{11,1... | collective-permute-start | bytes 1179656 | tf_op jit(solution)/shard_map/ppermute | solution.py:12
  14.7 12.1 %collective-permute-start.1 = (f32[5,128,128]{2,1,0:T(8,128)S(1)}, f32[5,128,128]{2,1,0:T(8,128)S(1)}, u32[]{:S(2)}, u32[]{:S(2)}) collective-permute-start(f32[5,128,128]{2,1,0:T(8,128)S(1)} %slice.655), channel_id=1, source_target_pairs={{31,0},{0,1},{1,2},{2,3},{3,4},{4,5},{5,6},{6,7},{7,8},{8,9},{9,10... | collective-permute-start | bytes 983048 | tf_op jit(solution)/shard_map/ppermute | solution.py:12
  14.8 12.8 %collective-permute-start.7 = (f32[5,128,128]{2,1,0:T(8,128)S(1)}, f32[5,128,128]{2,1,0:T(8,128)S(1)}, u32[]{:S(2)}, u32[]{:S(2)}) collective-permute-start(f32[5,128,128]{2,1,0:T(8,128)S(1)} %slice.679), channel_id=1, source_target_pairs={{1,0},{2,1},{3,2},{4,3},{5,4},{6,5},{7,6},{8,7},{9,8},{10,9},{11,1... | collective-permute-start | bytes 983048 | tf_op jit(solution)/shard_map/ppermute | solution.py:12
  26.8 10.5 %collective-permute-start.2 = (f32[4,128,128]{2,1,0:T(8,128)S(1)}, f32[4,128,128]{2,1,0:T(8,128)S(1)}, u32[]{:S(2)}, u32[]{:S(2)}) collective-permute-start(f32[4,128,128]{2,1,0:T(8,128)S(1)} %slice.656), channel_id=1, source_target_pairs={{31,0},{0,1},{1,2},{2,3},{3,4},{4,5},{5,6},{6,7},{7,8},{8,9},{9,10... | collective-permute-start | bytes 786440 | tf_op jit(solution)/shard_map/ppermute | solution.py:12
  27.6 9.8 %collective-permute-start.8 = (f32[4,128,128]{2,1,0:T(8,128)S(1)}, f32[4,128,128]{2,1,0:T(8,128)S(1)}, u32[]{:S(2)}, u32[]{:S(2)}) collective-permute-start(f32[4,128,128]{2,1,0:T(8,128)S(1)} %slice.688), channel_id=1, source_target_pairs={{1,0},{2,1},{3,2},{4,3},{5,4},{6,5},{7,6},{8,7},{9,8},{10,9},{11,1... | collective-permute-start | bytes 786440 | tf_op jit(solution)/shard_map/ppermute | solution.py:12
  37.3 8.9 %collective-permute-start.3 = (f32[3,128,128]{2,1,0:T(8,128)S(1)}, f32[3,128,128]{2,1,0:T(8,128)S(1)}, u32[]{:S(2)}, u32[]{:S(2)}) collective-permute-start(f32[3,128,128]{2,1,0:T(8,128)S(1)} %slice.657), channel_id=1, source_target_pairs={{31,0},{0,1},{1,2},{2,3},{3,4},{4,5},{5,6},{6,7},{7,8},{8,9},{9,10... | collective-permute-start | bytes 589832 | tf_op jit(solution)/shard_map/ppermute | solution.py:12
  37.4 8.9 %collective-permute-start.9 = (f32[3,128,128]{2,1,0:T(8,128)S(1)}, f32[3,128,128]{2,1,0:T(8,128)S(1)}, u32[]{:S(2)}, u32[]{:S(2)}) collective-permute-start(f32[3,128,128]{2,1,0:T(8,128)S(1)} %slice.695), channel_id=1, source_target_pairs={{1,0},{2,1},{3,2},{4,3},{5,4},{6,5},{7,6},{8,7},{9,8},{10,9},{11,1... | collective-permute-start | bytes 589832 | tf_op jit(solution)/shard_map/ppermute | solution.py:12
  46.3 8.1 %collective-permute-start.4 = (f32[2,128,128]{2,1,0:T(8,128)S(1)}, f32[2,128,128]{2,1,0:T(8,128)S(1)}, u32[]{:S(2)}, u32[]{:S(2)}) collective-permute-start(f32[2,128,128]{2,1,0:T(8,128)S(1)} %slice.658), channel_id=1, source_target_pairs={{31,0},{0,1},{1,2},{2,3},{3,4},{4,5},{5,6},{6,7},{7,8},{8,9},{9,10... | collective-permute-start | bytes 393224 | tf_op jit(solution)/shard_map/ppermute | solution.py:12
  46.4 8.1 %collective-permute-start.10 = (f32[2,128,128]{2,1,0:T(8,128)S(1)}, f32[2,128,128]{2,1,0:T(8,128)S(1)}, u32[]{:S(2)}, u32[]{:S(2)}) collective-permute-start(f32[2,128,128]{2,1,0:T(8,128)S(1)} %slice.700), channel_id=1, source_target_pairs={{1,0},{2,1},{3,2},{4,3},{5,4},{6,5},{7,6},{8,7},{9,8},{10,9},{11,1... | collective-permute-start | bytes 393224 | tf_op jit(solution)/shard_map/ppermute | solution.py:12
  54.4 7.4 %collective-permute-start.5 = (f32[1,128,128]{2,1,0:T(8,128)S(1)}, f32[1,128,128]{2,1,0:T(8,128)S(1)}, u32[]{:S(2)}, u32[]{:S(2)}) collective-permute-start(f32[1,128,128]{2,1,0:T(8,128)S(1)} %slice.659), channel_id=1, source_target_pairs={{31,0},{0,1},{1,2},{2,3},{3,4},{4,5},{5,6},{6,7},{7,8},{8,9},{9,10... | collective-permute-start | bytes 196616 | tf_op jit(solution)/shard_map/ppermute | solution.py:12
  54.5 9.3 %collective-permute-start.11 = (f32[1,128,128]{2,1,0:T(8,128)S(1)}, f32[1,128,128]{2,1,0:T(8,128)S(1)}, u32[]{:S(2)}, u32[]{:S(2)}) collective-permute-start(f32[1,128,128]{2,1,0:T(8,128)S(1)} %slice.701), channel_id=1, source_target_pairs={{1,0},{2,1},{3,2},{4,3},{5,4},{6,5},{7,6},{8,7},{9,8},{10,9},{11,1... | collective-permute-start | bytes 196616 | tf_op jit(solution)/shard_map/ppermute | solution.py:12
  66.8 14.8 %collective-permute-start.18 = (f32[6,128,128]{2,1,0:T(8,128)S(1)}, f32[6,128,128]{2,1,0:T(8,128)S(1)}, u32[]{:S(2)}, u32[]{:S(2)}) collective-permute-start(f32[6,128,128]{2,1,0:T(8,128)S(1)} %get-tuple-element.5), channel_id=1, source_target_pairs={{1,0},{2,1},{3,2},{4,3},{5,4},{6,5},{7,6},{8,7},{9,8},{10,9},{11,1... | collective-permute-start | bytes 1179656 | tf_op jit(solution)/shard_map/ppermute | solution.py:12
  70.6 10.9 %collective-permute-start.12 = (f32[6,128,128]{2,1,0:T(8,128)S(1)}, f32[6,128,128]{2,1,0:T(8,128)S(1)}, u32[]{:S(2)}, u32[]{:S(2)}) collective-permute-start(f32[6,128,128]{2,1,0:T(8,128)S(1)} %get-tuple-element.6), channel_id=1, source_target_pairs={{31,0},{0,1},{1,2},{2,3},{3,4},{4,5},{5,6},{6,7},{7,8},{8,9},{9,10... | collective-permute-start | bytes 1179656 | tf_op jit(solution)/shard_map/ppermute | solution.py:12
  81.5 10.3 %collective-permute-start.13 = (f32[5,128,128]{2,1,0:T(8,128)S(1)}, f32[5,128,128]{2,1,0:T(8,128)S(1)}, u32[]{:S(2)}, u32[]{:S(2)}) collective-permute-start(f32[5,128,128]{2,1,0:T(8,128)S(1)} %slice.704), channel_id=1, source_target_pairs={{31,0},{0,1},{1,2},{2,3},{3,4},{4,5},{5,6},{6,7},{7,8},{8,9},{9,10... | collective-permute-start | bytes 983048 | tf_op jit(solution)/shard_map/ppermute | solution.py:12
  81.7 10.6 %collective-permute-start.19 = (f32[5,128,128]{2,1,0:T(8,128)S(1)}, f32[5,128,128]{2,1,0:T(8,128)S(1)}, u32[]{:S(2)}, u32[]{:S(2)}) collective-permute-start(f32[5,128,128]{2,1,0:T(8,128)S(1)} %slice.736), channel_id=1, source_target_pairs={{1,0},{2,1},{3,2},{4,3},{5,4},{6,5},{7,6},{8,7},{9,8},{10,9},{11,1... | collective-permute-start | bytes 983048 | tf_op jit(solution)/shard_map/ppermute | solution.py:12
  91.8 9.6 %collective-permute-start.14 = (f32[4,128,128]{2,1,0:T(8,128)S(1)}, f32[4,128,128]{2,1,0:T(8,128)S(1)}, u32[]{:S(2)}, u32[]{:S(2)}) collective-permute-start(f32[4,128,128]{2,1,0:T(8,128)S(1)} %slice.705), channel_id=1, source_target_pairs={{31,0},{0,1},{1,2},{2,3},{3,4},{4,5},{5,6},{6,7},{7,8},{8,9},{9,10... | collective-permute-start | bytes 786440 | tf_op jit(solution)/shard_map/ppermute | solution.py:12
  92.3 9.6 %collective-permute-start.20 = (f32[4,128,128]{2,1,0:T(8,128)S(1)}, f32[4,128,128]{2,1,0:T(8,128)S(1)}, u32[]{:S(2)}, u32[]{:S(2)}) collective-permute-start(f32[4,128,128]{2,1,0:T(8,128)S(1)} %slice.745), channel_id=1, source_target_pairs={{1,0},{2,1},{3,2},{4,3},{5,4},{6,5},{7,6},{8,7},{9,8},{10,9},{11,1... | collective-permute-start | bytes 786440 | tf_op jit(solution)/shard_map/ppermute | solution.py:12
  101.4 8.9 %collective-permute-start.15 = (f32[3,128,128]{2,1,0:T(8,128)S(1)}, f32[3,128,128]{2,1,0:T(8,128)S(1)}, u32[]{:S(2)}, u32[]{:S(2)}) collective-permute-start(f32[3,128,128]{2,1,0:T(8,128)S(1)} %slice.706), channel_id=1, source_target_pairs={{31,0},{0,1},{1,2},{2,3},{3,4},{4,5},{5,6},{6,7},{7,8},{8,9},{9,10... | collective-permute-start | bytes 589832 | tf_op jit(solution)/shard_map/ppermute | solution.py:12
  101.9 8.8 %collective-permute-start.21 = (f32[3,128,128]{2,1,0:T(8,128)S(1)}, f32[3,128,128]{2,1,0:T(8,128)S(1)}, u32[]{:S(2)}, u32[]{:S(2)}) collective-permute-start(f32[3,128,128]{2,1,0:T(8,128)S(1)} %slice.752), channel_id=1, source_target_pairs={{1,0},{2,1},{3,2},{4,3},{5,4},{6,5},{7,6},{8,7},{9,8},{10,9},{11,1... | collective-permute-start | bytes 589832 | tf_op jit(solution)/shard_map/ppermute | solution.py:12
  110.3 8.0 %collective-permute-start.16 = (f32[2,128,128]{2,1,0:T(8,128)S(1)}, f32[2,128,128]{2,1,0:T(8,128)S(1)}, u32[]{:S(2)}, u32[]{:S(2)}) collective-permute-start(f32[2,128,128]{2,1,0:T(8,128)S(1)} %slice.707), channel_id=1, source_target_pairs={{31,0},{0,1},{1,2},{2,3},{3,4},{4,5},{5,6},{6,7},{7,8},{8,9},{9,10... | collective-permute-start | bytes 393224 | tf_op jit(solution)/shard_map/ppermute | solution.py:12
  110.7 8.1 %collective-permute-start.22 = (f32[2,128,128]{2,1,0:T(8,128)S(1)}, f32[2,128,128]{2,1,0:T(8,128)S(1)}, u32[]{:S(2)}, u32[]{:S(2)}) collective-permute-start(f32[2,128,128]{2,1,0:T(8,128)S(1)} %slice.757), channel_id=1, source_target_pairs={{1,0},{2,1},{3,2},{4,3},{5,4},{6,5},{7,6},{8,7},{9,8},{10,9},{11,1... | collective-permute-start | bytes 393224 | tf_op jit(solution)/shard_map/ppermute | solution.py:12
  118.4 7.3 %collective-permute-start.17 = (f32[1,128,128]{2,1,0:T(8,128)S(1)}, f32[1,128,128]{2,1,0:T(8,128)S(1)}, u32[]{:S(2)}, u32[]{:S(2)}) collective-permute-start(f32[1,128,128]{2,1,0:T(8,128)S(1)} %slice.708), channel_id=1, source_target_pairs={{31,0},{0,1},{1,2},{2,3},{3,4},{4,5},{5,6},{6,7},{7,8},{8,9},{9,10... | collective-permute-start | bytes 196616 | tf_op jit(solution)/shard_map/ppermute | solution.py:12
  118.7 8.8 %collective-permute-start.23 = (f32[1,128,128]{2,1,0:T(8,128)S(1)}, f32[1,128,128]{2,1,0:T(8,128)S(1)}, u32[]{:S(2)}, u32[]{:S(2)}) collective-permute-start(f32[1,128,128]{2,1,0:T(8,128)S(1)} %slice.758), channel_id=1, source_target_pairs={{1,0},{2,1},{3,2},{4,3},{5,4},{6,5},{7,6},{8,7},{9,8},{10,9},{11,1... | collective-permute-start | bytes 196616 | tf_op jit(solution)/shard_map/ppermute | solution.py:12
  (2 other events, 8.4 us)
where the time goes:
time: 130 us
  starting transfers between devices  65.8 us (51%)
  matrix products  34.8 us (27%)
  waiting for transfers between devices  24.9 us (19%)
  local copies, waits for them, and re-layouts  2.27 us (2%)
    ppermute x24, starting transfers between devices, from_behind(): return lax.ppermute(block, axis, route)  65.8 us
    dot_general x140, matrix products, band_product(): lax.dot_general(left_block, right_block, (((left_dim,), (right_dim,)), ((...  34.8 us
    ppermute x24, waiting for transfers between devices, from_behind(): return lax.ppermute(block, axis, route)  24.9 us
  transfers between devices with their start and end apart: 24, of which 15 were waited for; matrix products, arithmetic and copies ran while one was open for 24% of the time, Pallas kernels for 0%

commit v1 on v0

v1 whole, which is shorter than its diff:
```python
import functools

import jax
import jax.numpy as jnp
from jax import lax
from jax.experimental import pallas as pl
from jax.experimental.pallas import tpu as pltpu
from jax.sharding import PartitionSpec as P

REACH = 6
SLOTS = REACH + 1
MESH = pl.DeviceIdType.MESH
NN = (((1,), (0,)), ((), ()))
NT = (((1,), (1,)), ((), ()))


def split(value):
    high = value.astype(jnp.bfloat16)
    low = (value - high.astype(jnp.float32)).astype(jnp.bfloat16)
    return high, low


def side(blocks):
    return blocks[0] if len(blocks) == 1 else jnp.concatenate(blocks, axis=1)


def times(left, right):
    lh, ll = left
    rh, rl = right
    return lax.dot_general(
        jnp.concatenate([lh, ll, lh], axis=1),
        jnp.concatenate([rh, rh, rl], axis=0),
        NN,
        preferred_element_type=jnp.float32,
    )


def times_transposed(left, right):
    lh, ll = left
    rh, rl = right
    return lax.dot_general(
        jnp.concatenate([lh, ll, lh], axis=1),
        jnp.concatenate([rh, rh, rl], axis=1),
        NT,
        preferred_element_type=jnp.float32,
    )


def ready(slot):
    return max(slot, REACH - slot)


def kernel(
    rows,
    cols,
    own,
    pattern,
    out,
    up_p,
    down_p,
    up_s,
    down_s,
    square,
    cube,
    own_high,
    own_low,
    left_high,
    left_low,
    p_send,
    p_recv,
    s_send,
    s_recv,
):
    total = rows * cols
    me = lax.axis_index("row") * cols + lax.axis_index("col")

    def device(index):
        return (index // cols, lax.rem(index, cols))

    right = device(lax.rem(me + 1, total))
    left = device(lax.rem(me + total - 1, total))

    def p_right(hop):
        slots = pl.ds(hop, SLOTS - hop)
        return pltpu.make_async_remote_copy(
            src_ref=own.at[0, slots] if hop == 1 else up_p.at[hop - 2, slots],
            dst_ref=up_p.at[hop - 1, slots],
            send_sem=p_send.at[0, hop - 1],
            recv_sem=p_recv.at[0, hop - 1],
            device_id=right,
            device_id_type=MESH,
        )

    def p_left(hop):
        slots = pl.ds(0, SLOTS - hop)
        return pltpu.make_async_remote_copy(
            src_ref=own.at[0, slots] if hop == 1 else down_p.at[hop - 2, slots],
            dst_ref=down_p.at[hop - 1, slots],
            send_sem=p_send.at[1, hop - 1],
            recv_sem=p_recv.at[1, hop - 1],
            device_id=left,
            device_id_type=MESH,
        )

    def s_right(hop, slot):
        return pltpu.make_async_remote_copy(
            src_ref=square.at[slot] if hop == 1 else up_s.at[hop - 2, slot],
            dst_ref=up_s.at[hop - 1, slot],
            send_sem=s_send.at[0, hop - 1, slot],
            recv_sem=s_recv.at[0, hop - 1, slot],
            device_id=right,
            device_id_type=MESH,
        )

    def s_left(hop, slot):
        return pltpu.make_async_remote_copy(
            src_ref=square.at[slot] if hop == 1 else down_s.at[hop - 2, slot],
            dst_ref=down_s.at[hop - 1, slot],
            send_sem=s_send.at[1, hop - 1, slot],
            recv_sem=s_recv.at[1, hop - 1, slot],
            device_id=left,
            device_id_type=MESH,
        )

    barrier = pltpu.get_barrier_semaphore()
    for neighbour in (left, right):
        pl.semaphore_signal(barrier, inc=1, device_id=neighbour, device_id_type=MESH)
    pl.semaphore_wait(barrier, 2)

    p_right(1).start()
    p_left(1).start()

    flags = []
    for slot in range(SLOTS):
        column = lax.rem(me + slot, total)
        listed = jnp.int32(0)
        for place in range(pattern.shape[1]):
            listed = listed | (pattern[0, place] == column).astype(jnp.int32)
        flags.append(listed.astype(jnp.float32))

    for slot in range(SLOTS):
        high, low = split(own[0, slot])
        own_high[slot] = high
        own_low[slot] = low

    def own_pair(first, last):
        return (
            side([own_high[i] for i in range(first, last)]),
            side([own_low[i] for i in range(first, last)]),
        )

    def add(target, first, value):
        for i in range(value.shape[1] // 128):
            target[first + i] += value[:, i * 128 : (i + 1) * 128]

    def local(target, band_high_low):
        band = band_high_low
        value = times(own_pair(0, 1), band)
        for i in range(SLOTS):
            target[i] = value[:, i * 128 : (i + 1) * 128]
        rest = (band[0][:, 128:], band[1][:, 128:])
        target[0] += times_transposed(own_pair(1, SLOTS), rest)

    def from_up(target, buffer, hop):
        value = split(side([buffer[hop - 1, i] for i in range(hop, SLOTS)]))
        add(target, 0, times((left_high[hop - 1], left_low[hop - 1]), value))

    def from_down(target, buffer, hop):
        value = split(side([buffer[hop - 1, i] for i in range(SLOTS - hop)]))
        add(target, hop, times(own_pair(hop, hop + 1), value))
        if hop < REACH:
            rest = (value[0][:, 128:], value[1][:, 128:])
            add(target, hop, times_transposed(own_pair(hop + 1, SLOTS), rest))

    local(square, own_pair(0, SLOTS))

    for step in range(1, 2 * REACH + 1):
        if step <= REACH:
            p_right(step).wait_recv()
            if step < REACH:
                p_right(step + 1).start()
            p_left(step).wait_recv()
            if step < REACH:
                p_left(step + 1).start()
        for hop in range(REACH, 0, -1):
            for slot in range(SLOTS):
                if ready(slot) + hop != step:
                    continue
                if hop <= slot:
                    s_right(hop, slot).wait_recv()
                    if hop < slot:
                        s_right(hop + 1, slot).start()
                if hop <= REACH - slot:
                    s_left(hop, slot).wait_recv()
                    if hop < REACH - slot:
                        s_left(hop + 1, slot).start()
        if step <= REACH:
            high, low = split(up_p[step - 1, step].T)
            left_high[step - 1] = high
            left_low[step - 1] = low
            from_up(square, up_p, step)
            from_down(square, down_p, step)
            for slot in range(SLOTS):
                if ready(slot) == step:
                    square[slot] = square[slot] * flags[slot]
                    if slot >= 1:
                        s_right(1, slot).start()
                    if slot < REACH:
                        s_left(1, slot).start()
            if step == REACH:
                local(cube, split(side([square[i] for i in range(SLOTS)])))
        else:
            from_up(cube, up_s, step - REACH)
            from_down(cube, down_s, step - REACH)

    for slot in range(SLOTS):
        out[0, slot] = 3.0 * square[slot] - (2.0 * flags[slot]) * cube[slot]

    for hop in range(1, REACH + 1):
        p_right(hop).wait_send()
        p_left(hop).wait_send()
        for slot in range(SLOTS):
            if hop <= slot:
                s_right(hop, slot).wait_send()
            if hop <= REACH - slot:
                s_left(hop, slot).wait_send()


def solution(mesh):
    rows, cols = mesh.shape["row"], mesh.shape["col"]

    def on_device(density, pattern):
        halo = pltpu.VMEM((REACH, SLOTS, 128, 128), jnp.float32)
        band = pltpu.VMEM((SLOTS, 128, 128), jnp.float32)
        return pl.pallas_call(
            functools.partial(kernel, rows, cols),
            out_shape=jax.ShapeDtypeStruct(density.shape, jnp.float32),
            in_specs=[
                pl.BlockSpec(memory_space=pltpu.VMEM),
                pl.BlockSpec(memory_space=pltpu.SMEM),
            ],
            out_specs=pl.BlockSpec(memory_space=pltpu.VMEM),
            scratch_shapes=[
                halo,
                halo,
                halo,
                halo,
                band,
                band,
                pltpu.VMEM((SLOTS, 128, 128), jnp.bfloat16),
                pltpu.VMEM((SLOTS, 128, 128), jnp.bfloat16),
                pltpu.VMEM((REACH, 128, 128), jnp.bfloat16),
                pltpu.VMEM((REACH, 128, 128), jnp.bfloat16),
                pltpu.SemaphoreType.DMA((2, REACH)),
                pltpu.SemaphoreType.DMA((2, REACH)),
                pltpu.SemaphoreType.DMA((2, REACH, SLOTS)),
                pltpu.SemaphoreType.DMA((2, REACH, SLOTS)),
            ],
            compiler_params=pltpu.CompilerParams(
                collective_id=0, has_side_effects=True, vmem_limit_bytes=40 * 1024 * 1024
            ),
            cost_estimate=pl.CostEstimate(
                flops=140 * 2 * 128**3, bytes_accessed=14 * 4 * 128**2, transcendentals=0
            ),
        )(density, pattern)

    return jax.shard_map(
        on_device,
        mesh=mesh,
        in_specs=(P(("row", "col"), None, None, None), P(("row", "col"), None)),
        out_specs=P(("row", "col"), None, None, None),
        check_vma=False,
    )
```

time: 130 us -> 83.3 us (0.64)
  Pallas kernels: 0 us -> 80.7 us
  starting transfers between devices: 65.8 us -> 0 us
  matrix products: 34.8 us -> 0 us
  waiting for transfers between devices: 24.9 us -> 0 us
    pallas_call x0 -> x1, Pallas kernels: none -> 80.7 us  [on_device(): pl.pallas_call(functools.partial(kernel, rows, cols), out_shape=jax.Shape...]
    ppermute x24 -> x0, starting transfers between devices: 65.8 us -> none  [from_behind(): return lax.ppermute(block, axis, route)]
    dot_general x140 -> x0, matrix products: 34.8 us -> none  [band_product(): lax.dot_general(left_block, right_block, (((left_dim,), (right_dim,)), ((...]
    ppermute x24 -> x0, waiting for transfers between devices: 24.9 us -> none  [from_behind(): return lax.ppermute(block, axis, route)]
    unnamed x10 -> x5, local copies, waits for them, and re-layouts: 0.7 us -> 2.44 us
    slice x22 -> x0, local copies, waits for them, and re-layouts: 1.57 us -> none  [the longest x10 1.42 us: fetch_rows(): downward = from_behind(downward[:REACH + 1 - distance], ('row', 'col'), -1)]
  transfers between devices with their start and end apart: 24 -> 0, of which waited for: 15 -> 0; matrix products, arithmetic and copies ran while one was open for 24% -> 0% of each run, Pallas kernels for 0% -> 0%
where the time goes in v1:
time: 83.3 us; the launch traced here: 83.2 us
  Pallas kernels  80.7 us (97%)
  local copies, waits for them, and re-layouts  2.44 us (3%)
    pallas_call x1, Pallas kernels, on_device(): pl.pallas_call(functools.partial(kernel, rows, cols), out_shape=jax.Shape...  80.7 us
    unnamed x5, local copies, waits for them, and re-layouts  2.44 us

profile of v1, /device:TPU:0, one launch (start us, length us, event | category | flops | bytes accessed | tf_op | source)
XLA Modules:
  0.0 83.2 jit_solution(13557798752489666724)
XLA Ops:
  0.0 0.0 copy-start
  0.0 1.0 %copy-done = f32[1,7,128,128]{3,2,1,0:T(8,128)S(1)} copy-done((f32[1,7,128,128]{3,2,1,0:T(8,128)S(1)}, f32[1,7,128,128]{3,2,1,0:T(8,128)}, u32[]{:S(2)}) %copy-start) | copy-done | bytes 458776
  1.0 0.0 copy-start.1
  1.0 0.7 copy-done.1
  1.7 80.7 %shard_map.28 = f32[1,7,128,128]{3,2,1,0:T(8,128)S(1)} custom-call(f32[1,7,128,128]{3,2,1,0:T(8,128)S(1)} %copy-done, s32[1,12]{1,0:T(1,128)S(1)} %copy-done.1), custom_call_target="tpu_custom_call" | custom-call | flops 587202560 | bytes 917504 | tf_op jit(solution)/shard_map/pallas_call | solution.py:235
  82.4 0.8 copy.4
Async XLA Ops:
  0.0 1.0 %copy-start = (f32[1,7,128,128]{3,2,1,0:T(8,128)S(1)}, f32[1,7,128,128]{3,2,1,0:T(8,128)}, u32[]{:S(2)}) copy-start(f32[1,7,128,128]{3,2,1,0:T(8,128)} %own.1) | copy-start | bytes 1376260
  1.0 0.7 copy-start.1

commit v2 on v1

--- a/solution.py
+++ b/solution.py
@@ -10,6 +10,7 @@
 REACH = 6
 SLOTS = REACH + 1
 MESH = pl.DeviceIdType.MESH
+FAR_FIRST = (6, 0, 5, 1, 4, 2, 3)
 NN = (((1,), (0,)), ((), ()))
 NT = (((1,), (1,)), ((), ()))
 
@@ -50,12 +51,40 @@
     return max(slot, REACH - slot)
 
 
+CYCLE = (0, 8, 9, 1, 5, 6, 7, 3, 2, 10, 11, 15, 14, 13, 12, 4)
+
+
+def look_up(table, index):
+    value = jnp.int32(0)
+    for place, entry in enumerate(table):
+        value = value + jnp.where(index == place, entry, 0)
+    return value
+
+
+def cycle_device(rows, cols, index):
+    if (rows, cols) == (4, 8):
+        index = 2 * look_up(CYCLE, index // 2) + lax.rem(index, 2)
+    return index // cols, lax.rem(index, cols)
+
+
+def cycle_row(rows, cols, line, place):
+    index = line * cols + place
+    if (rows, cols) == (4, 8):
+        chips = [CYCLE.index(chip) for chip in range(len(CYCLE))]
+        index = 2 * look_up(chips, index // 2) + lax.rem(index, 2)
+    return index
+
+
 def kernel(
     rows,
     cols,
-    own,
+    given,
     pattern,
     out,
+    own,
+    result,
+    given_flags,
+    flags,
     up_p,
     down_p,
     up_s,
@@ -70,34 +99,58 @@
     p_recv,
     s_send,
     s_recv,
+    swap_send,
+    swap_recv,
 ):
     total = rows * cols
-    me = lax.axis_index("row") * cols + lax.axis_index("col")
+    line, place = lax.axis_index("row"), lax.axis_index("col")
+    given_row = line * cols + place
+    me = cycle_row(rows, cols, line, place)
 
     def device(index):
-        return (index // cols, lax.rem(index, cols))
+        return cycle_device(rows, cols, index)
 
     right = device(lax.rem(me + 1, total))
     left = device(lax.rem(me + total - 1, total))
-
-    def p_right(hop):
-        slots = pl.ds(hop, SLOTS - hop)
-        return pltpu.make_async_remote_copy(
-            src_ref=own.at[0, slots] if hop == 1 else up_p.at[hop - 2, slots],
-            dst_ref=up_p.at[hop - 1, slots],
-            send_sem=p_send.at[0, hop - 1],
-            recv_sem=p_recv.at[0, hop - 1],
+    worker = device(given_row)
+    owner = (me // cols, lax.rem(me, cols))
+    moved = me != given_row
+
+    def move(source, target, kind, index, to):
+        return pltpu.make_async_remote_copy(
+            src_ref=source,
+            dst_ref=target,
+            send_sem=swap_send.at[kind, index],
+            recv_sem=swap_recv.at[kind, index],
+            device_id=to,
+            device_id_type=MESH,
+        )
+
+    def move_in(slot):
+        return move(given.at[0, slot], own.at[slot], 0, slot, worker)
+
+    def move_flags():
+        return move(given_flags, flags, 0, SLOTS, worker)
+
+    def move_out(slot):
+        return move(result.at[slot], out.at[0, slot], 1, slot, owner)
+
+    def p_right(hop, slot):
+        return pltpu.make_async_remote_copy(
+            src_ref=own.at[slot] if hop == 1 else up_p.at[hop - 2, slot],
+            dst_ref=up_p.at[hop - 1, slot],
+            send_sem=p_send.at[0, hop - 1, slot],
+            recv_sem=p_recv.at[0, hop - 1, slot],
             device_id=right,
             device_id_type=MESH,
         )
 
-    def p_left(hop):
-        slots = pl.ds(0, SLOTS - hop)
-        return pltpu.make_async_remote_copy(
-            src_ref=own.at[0, slots] if hop == 1 else down_p.at[hop - 2, slots],
-            dst_ref=down_p.at[hop - 1, slots],
-            send_sem=p_send.at[1, hop - 1],
-            recv_sem=p_recv.at[1, hop - 1],
+    def p_left(hop, slot):
+        return pltpu.make_async_remote_copy(
+            src_ref=own.at[slot] if hop == 1 else down_p.at[hop - 2, slot],
+            dst_ref=down_p.at[hop - 1, slot],
+            send_sem=p_send.at[1, hop - 1, slot],
+            recv_sem=p_recv.at[1, hop - 1, slot],
             device_id=left,
             device_id_type=MESH,
         )
@@ -125,21 +178,51 @@
     barrier = pltpu.get_barrier_semaphore()
     for neighbour in (left, right):
         pl.semaphore_signal(barrier, inc=1, device_id=neighbour, device_id_type=MESH)
-    pl.semaphore_wait(barrier, 2)
-
-    p_right(1).start()
-    p_left(1).start()
-
-    flags = []
+
+    @pl.when(moved)
+    def _():
+        for partner in (worker, owner):
+            pl.semaphore_signal(barrier, inc=1, device_id=partner, device_id_type=MESH)
+
     for slot in range(SLOTS):
-        column = lax.rem(me + slot, total)
+        column = lax.rem(given_row + slot, total)
         listed = jnp.int32(0)
-        for place in range(pattern.shape[1]):
-            listed = listed | (pattern[0, place] == column).astype(jnp.int32)
-        flags.append(listed.astype(jnp.float32))
+        for entry in range(pattern.shape[1]):
+            listed = listed | (pattern[0, entry] == column).astype(jnp.int32)
+        given_flags[slot : slot + 1, :] = jnp.full((1, 128), listed.astype(jnp.float32))
+    given_flags[SLOTS:, :] = jnp.zeros((1, 128), jnp.float32)
+
+    @pl.when(moved)
+    def _():
+        pl.semaphore_wait(barrier, 4)
+        for slot in FAR_FIRST:
+            move_in(slot).start()
+        move_flags().start()
+
+    @pl.when(jnp.logical_not(moved))
+    def _():
+        for slot in range(SLOTS):
+            own[slot] = given[0, slot]
+        flags[...] = given_flags[...]
+        pl.semaphore_wait(barrier, 2)
+
+    for slot in FAR_FIRST:
+
+        @pl.when(moved)
+        def _():
+            move_in(slot).wait_recv()
+
+        if slot >= 1:
+            p_right(1, slot).start()
+        if slot < REACH:
+            p_left(1, slot).start()
+
+    @pl.when(moved)
+    def _():
+        move_flags().wait_recv()
 
     for slot in range(SLOTS):
-        high, low = split(own[0, slot])
+        high, low = split(own[slot])
         own_high[slot] = high
         own_low[slot] = low
 
@@ -176,12 +259,13 @@
 
     for step in range(1, 2 * REACH + 1):
         if step <= REACH:
-            p_right(step).wait_recv()
-            if step < REACH:
-                p_right(step + 1).start()
-            p_left(step).wait_recv()
-            if step < REACH:
-                p_left(step + 1).start()
+            for slot in range(SLOTS - step):
+                p_right(step, REACH - slot).wait_recv()
+                if REACH - slot > step:
+                    p_right(step + 1, REACH - slot).start()
+                p_left(step, slot).wait_recv()
+                if slot < REACH - step:
+                    p_left(step + 1, slot).start()
         for hop in range(REACH, 0, -1):
             for slot in range(SLOTS):
                 if ready(slot) + hop != step:
@@ -202,7 +286,7 @@
             from_down(square, down_p, step)
             for slot in range(SLOTS):
                 if ready(slot) == step:
-                    square[slot] = square[slot] * flags[slot]
+                    square[slot] = square[slot] * flags[slot : slot + 1, :]
                     if slot >= 1:
                         s_right(1, slot).start()
                     if slot < REACH:
@@ -212,18 +296,34 @@
         else:
             from_up(cube, up_s, step - REACH)
             from_down(cube, down_s, step - REACH)
-
-    for slot in range(SLOTS):
-        out[0, slot] = 3.0 * square[slot] - (2.0 * flags[slot]) * cube[slot]
+            for slot in range(SLOTS):
+                if ready(slot) == step - REACH:
+                    twice = 2.0 * flags[slot : slot + 1, :]
+                    result[slot] = 3.0 * square[slot] - twice * cube[slot]
+
+                    @pl.when(moved)
+                    def _():
+                        move_out(slot).start()
+
+                    @pl.when(jnp.logical_not(moved))
+                    def _():
+                        out[0, slot] = result[slot]
 
     for hop in range(1, REACH + 1):
-        p_right(hop).wait_send()
-        p_left(hop).wait_send()
         for slot in range(SLOTS):
             if hop <= slot:
+                p_right(hop, slot).wait_send()
                 s_right(hop, slot).wait_send()
             if hop <= REACH - slot:
+                p_left(hop, slot).wait_send()
                 s_left(hop, slot).wait_send()
+
+    @pl.when(moved)
+    def _():
+        move_flags().wait_send()
+        for slot in range(SLOTS):
+            move_in(slot).wait_send()
+            move_out(slot).wait()
 
 
 def solution(mesh):
@@ -241,6 +341,10 @@
             ],
             out_specs=pl.BlockSpec(memory_space=pltpu.VMEM),
             scratch_shapes=[
+                band,
+                band,
+                pltpu.VMEM((SLOTS + 1, 128), jnp.float32),
+                pltpu.VMEM((SLOTS + 1, 128), jnp.float32),
                 halo,
                 halo,
                 halo,
@@ -251,10 +355,12 @@
                 pltpu.VMEM((SLOTS, 128, 128), jnp.bfloat16),
                 pltpu.VMEM((REACH, 128, 128), jnp.bfloat16),
                 pltpu.VMEM((REACH, 128, 128), jnp.bfloat16),
-                pltpu.SemaphoreType.DMA((2, REACH)),
-                pltpu.SemaphoreType.DMA((2, REACH)),
                 pltpu.SemaphoreType.DMA((2, REACH, SLOTS)),
                 pltpu.SemaphoreType.DMA((2, REACH, SLOTS)),
+                pltpu.SemaphoreType.DMA((2, REACH, SLOTS)),
+                pltpu.SemaphoreType.DMA((2, REACH, SLOTS)),
+                pltpu.SemaphoreType.DMA((2, SLOTS + 1)),
+                pltpu.SemaphoreType.DMA((2, SLOTS + 1)),
             ],
             compiler_params=pltpu.CompilerParams(
                 collective_id=0, has_side_effects=True, vmem_limit_bytes=40 * 1024 * 1024

time: 83.3 us -> 79.3 us (0.952)
  the two profiles are of different devices: /device:TPU:0 before, /device:TPU:22 now
where the time goes in v2:
time: 79.3 us; the launch traced here: 79.1 us
  Pallas kernels  76.7 us (97%)
  local copies, waits for them, and re-layouts  2.44 us (3%)
    pallas_call x1, Pallas kernels, on_device(): pl.pallas_call(functools.partial(kernel, rows, cols), out_shape=jax.Shape...  76.7 us
    unnamed x5, local copies, waits for them, and re-layouts  2.44 us

profile of v2, /device:TPU:22, one launch (start us, length us, event | category | flops | bytes accessed | tf_op | source)
XLA Modules:
  0.0 79.1 jit_solution(5025085728447771631)
XLA Ops:
  0.0 0.0 copy-start
  0.0 1.0 %copy-done = f32[1,7,128,128]{3,2,1,0:T(8,128)S(1)} copy-done((f32[1,7,128,128]{3,2,1,0:T(8,128)S(1)}, f32[1,7,128,128]{3,2,1,0:T(8,128)}, u32[]{:S(2)}) %copy-start) | copy-done | bytes 458776
  1.0 0.0 copy-start.1
  1.0 0.7 copy-done.1
  1.7 76.7 %shard_map.28 = f32[1,7,128,128]{3,2,1,0:T(8,128)S(1)} custom-call(f32[1,7,128,128]{3,2,1,0:T(8,128)S(1)} %copy-done, s32[1,12]{1,0:T(1,128)S(1)} %copy-done.1), custom_call_target="tpu_custom_call" | custom-call | flops 587202560 | bytes 917504 | tf_op jit(solution)/shard_map/pallas_call | solution.py:335
  78.4 0.8 copy.4
Async XLA Ops:
  0.0 1.0 %copy-start = (f32[1,7,128,128]{3,2,1,0:T(8,128)S(1)}, f32[1,7,128,128]{3,2,1,0:T(8,128)}, u32[]{:S(2)}) copy-start(f32[1,7,128,128]{3,2,1,0:T(8,128)} %given.1) | copy-start | bytes 1376260
  1.0 0.7 copy-start.1

commit v3 on v2

--- a/solution.py
+++ b/solution.py
@@ -10,7 +10,7 @@
 REACH = 6
 SLOTS = REACH + 1
 MESH = pl.DeviceIdType.MESH
-FAR_FIRST = (6, 0, 5, 1, 4, 2, 3)
+FAR_FIRST = (3, 2, 4, 1, 5, 0, 6)
 NN = (((1,), (0,)), ((), ()))
 NT = (((1,), (1,)), ((), ()))
 

time: 79.3 us -> 79 us (level)
  the two profiles are of different devices: /device:TPU:22 before, /device:TPU:8 now
where the time goes in v3:
time: 79 us; the launch traced here: 78.8 us
  Pallas kernels  76.4 us (97%)
  local copies, waits for them, and re-layouts  2.44 us (3%)
    pallas_call x1, Pallas kernels, on_device(): pl.pallas_call(functools.partial(kernel, rows, cols), out_shape=jax.Shape...  76.4 us
    unnamed x5, local copies, waits for them, and re-layouts  2.44 us

profile of v3, /device:TPU:8, one launch (start us, length us, event | category | flops | bytes accessed | tf_op | source)
XLA Modules:
  0.0 78.8 jit_solution(12467778517463655632)
XLA Ops:
  0.0 0.0 copy-start
  0.0 1.0 %copy-done = f32[1,7,128,128]{3,2,1,0:T(8,128)S(1)} copy-done((f32[1,7,128,128]{3,2,1,0:T(8,128)S(1)}, f32[1,7,128,128]{3,2,1,0:T(8,128)}, u32[]{:S(2)}) %copy-start) | copy-done | bytes 458776
  1.0 0.0 copy-start.1
  1.0 0.7 copy-done.1
  1.7 76.4 %shard_map.28 = f32[1,7,128,128]{3,2,1,0:T(8,128)S(1)} custom-call(f32[1,7,128,128]{3,2,1,0:T(8,128)S(1)} %copy-done, s32[1,12]{1,0:T(1,128)S(1)} %copy-done.1), custom_call_target="tpu_custom_call" | custom-call | flops 587202560 | bytes 917504 | tf_op jit(solution)/shard_map/pallas_call | solution.py:335
  78.0 0.8 copy.4
Async XLA Ops:
  0.0 1.0 %copy-start = (f32[1,7,128,128]{3,2,1,0:T(8,128)S(1)}, f32[1,7,128,128]{3,2,1,0:T(8,128)}, u32[]{:S(2)}) copy-start(f32[1,7,128,128]{3,2,1,0:T(8,128)} %given.1) | copy-start | bytes 1376260
  1.0 0.7 copy-start.1
